TPU v7x, 32 devices: a whole 2x2x4 slice. The times are simulated.
32 devices in a mesh: grp: 2 (over x), long: 16 (over z, y, core).
Axes of the slice: x: 2, y: 2, z: 4, core: 2. Of those that a mesh axis runs over, the one named last changes fastest.
Arguments:
- pixel_map: int32 [256, 2048], P(('grp', 'long')), parts along dimension 0, may hold values from 0 to 3
- materials: float32 [8], P('grp'), parts along dimension 0, may hold values from 1.5 to 12
- mode_panel: float32 [128, 2, 201, 201], P(('grp', 'long')), parts along dimension 0, may hold values from -1.6 to 1.6
Outputs:
- coupled_panel: float32 [128, 2, 201, 201], P(('grp', 'long')), parts along dimension 0
There are 2 independent parts, one for each index of `grp`. A program takes and returns all parts, laid end to end along the dimension named above; each array names one. Nothing has to cross between parts.
All inputs are finite; a program needn't handle non-finite values.
Results may differ from a plain program's by a relative error of at most 0.0003.
Values sent between devices are 32-bit elements; how exact they have to be, the bound alone decides.
A program may use at most 128 MiB of HBM per device.

v0:
```python
import functools

import jax
import jax.numpy as jnp
import ml_dtypes
import numpy as np
from jax import lax
from jax.experimental import pallas as pl
from jax.experimental.pallas import tpu as pltpu
from jax.sharding import PartitionSpec as P

NS_ITERS = 3
BLOCK = 128
VMEM_BYTES = 56 * 1024 * 1024


def round_up(value, step):
    return -(-value // step) * step


def split_table(table):
    high = table.astype(np.float32).astype(ml_dtypes.bfloat16)
    low = (table - high.astype(np.float64)).astype(ml_dtypes.bfloat16)
    return high, low


def turns(first, second, period):
    return np.mod(np.outer(first, second), period) * (2.0 * np.pi / period)


def symbol_table(orders, pixels):
    reach = orders - 1
    period = 2 * orders - 1
    lanes = round_up(orders, 2 * BLOCK)
    harmonics = np.arange(1, reach + 1)
    frequencies = np.arange(orders)
    by_frequency = turns(harmonics, frequencies, period)
    by_pixel = turns(np.arange(pixels), harmonics, pixels)
    table = np.zeros((pixels, 2 * lanes))
    table[:, :orders] = (1.0 + 2.0 * np.cos(by_pixel) @ np.cos(by_frequency)) / pixels
    table[:, lanes : lanes + orders] = -2.0 * np.sin(by_pixel) @ np.sin(by_frequency) / pixels
    return split_table(table)


def order_tables(orders):
    period = 2 * orders - 1
    lanes = round_up(orders, 2 * BLOCK)
    angle = turns(np.arange(orders) - (orders - 1) // 2, np.arange(orders), period)
    weight = np.where(np.arange(orders) == 0, 1.0, 2.0)[:, None] / period
    forward = np.zeros((lanes, 2 * lanes))
    forward[:orders, :orders] = np.cos(angle)
    forward[:orders, lanes : lanes + orders] = np.sin(angle)
    backward = np.zeros((2 * lanes, lanes))
    backward[:orders, :orders] = weight * np.cos(angle).T
    backward[lanes : lanes + orders, :orders] = weight * np.sin(angle).T
    even = backward[:lanes] @ forward[:, :lanes]
    odd = backward[lanes:] @ forward[:, lanes:]
    return split_table(forward), split_table(backward), split_table(even), split_table(odd)


def line_tables(y_orders, lines):
    kept = min(y_orders, lines)
    padded = round_up(kept, BLOCK)
    blocks = lines // BLOCK
    angle = turns(np.arange(lines), np.arange(kept) - (y_orders - 1) // 2, lines)
    cosine = np.zeros((blocks, BLOCK, padded))
    sine = np.zeros((blocks, BLOCK, padded))
    cosine[:, :, :kept] = np.cos(angle).reshape(blocks, BLOCK, kept)
    sine[:, :, :kept] = np.sin(angle).reshape(blocks, BLOCK, kept)
    real = np.concatenate([cosine, -sine], axis=2)
    imag = np.concatenate([sine, cosine], axis=2)
    spread = np.stack([real, imag], axis=1).reshape(2 * lines, 2 * padded)
    return split_table(spread), split_table(spread.T / lines)


def split(value):
    high = value.astype(jnp.bfloat16)
    return high, (value - high.astype(jnp.float32)).astype(jnp.bfloat16)


def mul(left, right):
    return jnp.dot(left, right, preferred_element_type=jnp.float32)


def mul_table(high, low, table_high, table_low):
    return mul(high, table_high) + mul(low, table_high) + mul(high, table_low)


def scale_of(materials, shape):
    values = [jnp.full(shape, materials[i], jnp.float32) for i in range(materials.shape[0])]
    least = functools.reduce(jnp.minimum, values)
    most = functools.reduce(jnp.maximum, values)
    return 2.0 / (1.0 / least + 1.0 / most)


def symbol_kernel(materials, pixel_rows, table_high, table_low, symbol):
    pixels = pixel_rows[...]
    count = pixels.shape[0]
    inverse_eps = jnp.zeros(pixels.shape, jnp.float32)
    for i in range(materials.shape[0]):
        inverse = 1.0 / jnp.full(pixels.shape, materials[i], jnp.float32)
        inverse_eps = jnp.where(pixels == i, inverse, inverse_eps)
    high, low = split(inverse_eps)
    rows = jnp.concatenate([high, low], axis=0)
    sums = mul(rows, table_high[...]) + mul(rows, table_low[...])
    sums = sums[:count] + sums[count:]
    lanes = sums.shape[1] // 2
    scaled = scale_of(materials, sums.shape) * sums
    symbol[:, :lanes] = 1.0 - scaled[:, :lanes]
    symbol[:, lanes:] = -scaled[:, lanes:]


def panel_kernel(
    materials,
    panel,
    symbol,
    spread_high,
    spread_low,
    gather_high,
    gather_low,
    forward_high,
    forward_low,
    backward_high,
    backward_low,
    even_high,
    even_low,
    odd_high,
    odd_low,
    out,
    folded,
    spread,
    start,
    state,
    high_side,
    low_side,
):
    columns, _, y_orders, orders = panel.shape
    lines, width = symbol.shape
    lanes = width // 2
    blocks = lines // BLOCK
    unit = 2 * BLOCK
    units = columns * blocks
    group = 2 if units % 2 == 0 else 1
    kept = min(y_orders, lines)
    padded = spread_high.shape[1] // 2

    folded[...] = jnp.zeros(folded.shape, jnp.float32)
    for c in range(columns):
        for part in range(2):
            base = part * padded
            folded[c, base : base + kept, :orders] = panel[c, part, :kept, :]
            for first in range(kept, y_orders, kept):
                size = min(kept, y_orders - first)
                folded[c, base : base + size, :orders] += panel[c, part, first : first + size, :]
        high, low = split(folded[c])
        spread[c * 2 * lines : (c + 1) * 2 * lines, :] = (
            mul(spread_high[...], high) + mul(spread_high[...], low) + mul(spread_low[...], high)
        )

    for g in range(0, units, group):
        rows = slice(g * unit, (g + group) * unit)
        high, low = split(spread[rows, :])
        value = mul_table(high, low, forward_high[...], forward_low[...])
        start[rows, :] = value
        state[rows, :] = value

    def weigh(u):
        real = slice(u * unit, u * unit + BLOCK)
        imag = slice(u * unit + BLOCK, (u + 1) * unit)
        here = slice((u % blocks) * BLOCK, (u % blocks + 1) * BLOCK)
        p = symbol[here, :lanes]
        q = symbol[here, lanes:]
        even_real = state[real, :lanes]
        even_imag = state[imag, :lanes]
        odd_real = state[real, lanes:]
        odd_imag = state[imag, lanes:]
        for rows, cols, value in (
            (real, slice(0, lanes), p * even_real + q * odd_imag),
            (imag, slice(0, lanes), p * even_imag - q * odd_real),
            (real, slice(lanes, width), p * odd_real - q * even_imag),
            (imag, slice(lanes, width), p * odd_imag + q * even_real),
        ):
            high, low = split(value)
            high_side[rows, cols] = high
            low_side[rows, cols] = low

    def sweep(_, carry):
        for g in range(0, units, group):
            rows = slice(g * unit, (g + group) * unit)
            for u in range(g, g + group):
                weigh(u)
            state[rows, :lanes] = start[rows, :lanes] + mul_table(
                high_side[rows, :lanes], low_side[rows, :lanes], even_high[...], even_low[...]
            )
            state[rows, lanes:] = start[rows, lanes:] + mul_table(
                high_side[rows, lanes:], low_side[rows, lanes:], odd_high[...], odd_low[...]
            )
        return carry

    lax.fori_loop(0, 2**NS_ITERS - 2, sweep, 0)

    scale = scale_of(materials, (1, lanes))
    for g in range(0, units, group):
        rows = slice(g * unit, (g + group) * unit)
        for u in range(g, g + group):
            weigh(u)
        spread[rows, :] = scale * (
            spread[rows, :]
            + mul_table(high_side[rows, :], low_side[rows, :], backward_high[...], backward_low[...])
        )

    for c in range(columns):
        high, low = split(spread[c * 2 * lines : (c + 1) * 2 * lines, :])
        value = (
            mul(gather_high[...], high) + mul(gather_high[...], low) + mul(gather_low[...], high)
        )
        for part in range(2):
            base = part * padded
            for first in range(0, y_orders, kept):
                size = min(kept, y_orders - first)
                out[c, part, first : first + size, :] = value[base : base + size, :orders]


def whole(count):
    return [pl.BlockSpec(memory_space=pltpu.VMEM)] * count


def local(pixel_map, materials, mode_panel):
    rows, pixels = pixel_map.shape
    columns, _, y_orders, orders = mode_panel.shape
    lines = rows * lax.axis_size("long")
    lanes = round_up(orders, 2 * BLOCK)
    width = 2 * lanes
    scalars = pl.BlockSpec(memory_space=pltpu.SMEM)
    params = pltpu.CompilerParams(vmem_limit_bytes=VMEM_BYTES)
    symbol = pl.pallas_call(
        symbol_kernel,
        out_shape=jax.ShapeDtypeStruct((rows, width), jnp.float32),
        in_specs=[scalars] + whole(3),
        out_specs=pl.BlockSpec(memory_space=pltpu.VMEM),
        compiler_params=params,
        name="symbol",
    )(materials, pixel_map, *map(jnp.asarray, symbol_table(orders, pixels)))
    symbol = lax.all_gather(symbol, "long", axis=0, tiled=True)
    spread_table, gather_table = line_tables(y_orders, lines)
    forward, backward, even, odd = order_tables(orders)
    tables = [*spread_table, *gather_table, *forward, *backward, *even, *odd]
    total = columns * 2 * lines
    folded_rows = spread_table[0].shape[1]
    return pl.pallas_call(
        panel_kernel,
        out_shape=jax.ShapeDtypeStruct(mode_panel.shape, jnp.float32),
        in_specs=[scalars] + whole(2 + len(tables)),
        out_specs=pl.BlockSpec(memory_space=pltpu.VMEM),
        scratch_shapes=[
            pltpu.VMEM((columns, folded_rows, lanes), jnp.float32),
            pltpu.VMEM((total, lanes), jnp.float32),
            pltpu.VMEM((total, width), jnp.float32),
            pltpu.VMEM((total, width), jnp.float32),
            pltpu.VMEM((total, width), jnp.bfloat16),
            pltpu.VMEM((total, width), jnp.bfloat16),
        ],
        compiler_params=params,
        name="panel",
    )(materials, mode_panel, symbol, *map(jnp.asarray, tables))


def solution(mesh):
    in_specs = (P(("grp", "long"), None), P("grp"), P(("grp", "long"), None, None, None))
    out_specs = P(("grp", "long"), None, None, None)
    return jax.shard_map(local, mesh=mesh, in_specs=in_specs, out_specs=out_specs, check_vma=False)
```

profile of v0, /device:TPU:1, one launch (start us, length us, event | category | flops | bytes accessed | tf_op | source)
XLA Modules:
  0.0 47.3 jit_solution(12446658319013615228)
XLA Ops:
  0.0 0.0 copy-start
  0.0 3.6 %symbol.1 = f32[8,512]{1,0:T(8,128)} custom-call(f32[4]{0:T(128)} %materials.3, s32[8,2048]{1,0:T(8,128)} %pixel_rows.1, bf16[2048,512]{1,0:T(8,128)(2,1)} %constant.28.clone.table_high, bf16[2048,512]{1,0:T(8,128)(2,1)} %constant.29.clone.table_low), custom_call_target="tpu_custom_call" | custom-call | tf_op jit(solution)/shard_map/symbol/pallas_call | solution.py:236
  3.6 25.3 %all_gather.3.symbol = f32[128,512]{1,0:T(8,128)} all-gather(f32[8,512]{1,0:T(8,128)} %symbol.1), channel_id=1, replica_groups=mesh['grp'=2,'long'=16] {'long'}, dimensions={0}, use_global_device_ids=true | all-gather | bytes 278528 | tf_op jit(solution)/shard_map/all_gather | solution.py:244
  29.0 0.0 copy-done
  29.0 1.4 %copy.18.panel = f32[4,2,201,201]{3,2,1,0:T(8,128)} copy(f32[4,2,201,201]{3,1,2,0:T(2,128)S(1)} %copy-done) | data formatting | bytes 2585664 | tf_op args[2]
  30.3 13.1 %panel.2 = f32[4,2,201,201]{3,2,1,0:T(8,128)} custom-call(f32[4]{0:T(128)} %materials.3, f32[4,2,201,201]{3,2,1,0:T(8,128)} %copy.18.panel, f32[128,512]{1,0:T(8,128)} %all_gather.3.symbol, bf16[256,256]{1,0:T(8,128)(2,1)} %constant.30.clone.spread_high, bf16[256,256]{1,0:T(8,128)(2,1)} %constant.31.clone.spread_low, ...), custom_call_target="tpu_custom_call" | custom-call | tf_op jit(solution)/shard_map/panel/pallas_call | solution.py:250
  43.4 3.9 %copy.19 = f32[4,2,201,201]{3,1,2,0:T(2,128)} copy(f32[4,2,201,201]{3,2,1,0:T(8,128)} %panel.2) | data formatting | bytes 2585664 | tf_op jit(solution)/shard_map/panel/pallas_call | solution.py:250
Async XLA Ops:
  0.0 29.0 %copy-start = (f32[4,2,201,201]{3,1,2,0:T(2,128)S(1)}, f32[4,2,201,201]{3,1,2,0:T(2,128)}, u32[]{:S(2)}) copy-start(f32[4,2,201,201]{3,1,2,0:T(2,128)} %param.19) | copy-start | bytes 3878500
where the time goes:
time: 47.6 us; the launch traced here: 47.3 us
  blocking collectives  25.3 us (53%)
  Pallas kernels  16.7 us (35%)
  local copies, waits for them, and re-layouts  5.25 us (11%)
    all_gather x1, blocking collectives, local(): symbol = lax.all_gather(symbol, 'long', axis=0, tiled=True)  25.3 us
    pallas_call x1, Pallas kernels, local(): pl.pallas_call(panel_kernel, out_shape=jax.ShapeDtypeStruct(mode_panel.sh...  13.1 us
    pallas_call x1, local copies, waits for them, and re-layouts, local(): pl.pallas_call(panel_kernel, out_shape=jax.ShapeDtypeStruct(mode_panel.sh...  3.89 us
    pallas_call x1, Pallas kernels, local(): pl.pallas_call(symbol_kernel, out_shape=jax.ShapeDtypeStruct((rows, width...  3.64 us
    unnamed x3, local copies, waits for them, and re-layouts  1.36 us

commit v1 on v0

--- a/solution.py
+++ b/solution.py
@@ -11,7 +11,8 @@
 
 NS_ITERS = 3
 BLOCK = 128
-VMEM_BYTES = 56 * 1024 * 1024
+CHUNKS = 4
+VMEM_BYTES = 28 * 1024 * 1024
 
 
 def round_up(value, step):
@@ -93,33 +94,115 @@
     return 2.0 / (1.0 / least + 1.0 / most)
 
 
-def symbol_kernel(materials, pixel_rows, table_high, table_low, symbol):
-    pixels = pixel_rows[...]
-    count = pixels.shape[0]
+def symbol_of(materials, pixels, tables, fetched, sums):
     inverse_eps = jnp.zeros(pixels.shape, jnp.float32)
     for i in range(materials.shape[0]):
         inverse = 1.0 / jnp.full(pixels.shape, materials[i], jnp.float32)
         inverse_eps = jnp.where(pixels == i, inverse, inverse_eps)
     high, low = split(inverse_eps)
     rows = jnp.concatenate([high, low], axis=0)
-    sums = mul(rows, table_high[...]) + mul(rows, table_low[...])
-    sums = sums[:count] + sums[count:]
-    lanes = sums.shape[1] // 2
-    scaled = scale_of(materials, sums.shape) * sums
-    symbol[:, :lanes] = 1.0 - scaled[:, :lanes]
-    symbol[:, lanes:] = -scaled[:, lanes:]
+    count = pixels.shape[0]
+    total = jnp.zeros((2 * count, tables[0].shape[1]), jnp.float32)
+    depth = rows.shape[1] // len(fetched)
+    for i, copies in enumerate(fetched):
+        part = slice(i * depth, (i + 1) * depth)
+        for copy, table in zip(copies, tables):
+            copy.wait()
+            total += mul(rows[:, part], table[part, :])
+    total = total[:count] + total[count:]
+    lanes = total.shape[1] // 2
+    scaled = scale_of(materials, total.shape) * total
+    sums[:, :lanes] = 1.0 - scaled[:, :lanes]
+    sums[:, lanes:] = -scaled[:, lanes:]
+
+
+def gather_kernel(
+    materials,
+    pixel_rows,
+    panel,
+    spread_high,
+    spread_low,
+    forward_high,
+    forward_low,
+    table_high,
+    table_low,
+    symbol,
+    spread,
+    start,
+    high_table,
+    low_table,
+    landed,
+    folded,
+    fetch_sem,
+    send_sem,
+    recv_sem,
+):
+    me = lax.axis_index("long")
+    devices = lax.axis_size("long")
+    barrier = pltpu.get_barrier_semaphore()
+    for i in range(1, devices):
+        pl.semaphore_signal(barrier, inc=1, device_id={"long": lax.rem(me + i, devices)})
+    pixels = pixel_rows[...]
+    depth = table_high.shape[0] // CHUNKS
+    fetched = []
+    for i in range(CHUNKS):
+        part = pl.ds(i * depth, depth)
+        copies = [
+            pltpu.make_async_copy(source.at[part], target.at[part], fetch_sem.at[2 * i + j])
+            for j, (source, target) in enumerate(((table_high, high_table), (table_low, low_table)))
+        ]
+        for copy in copies:
+            copy.start()
+        fetched.append(copies)
+    count = pixels.shape[0]
+    mine = landed.at[pl.ds(pl.multiple_of(me * count, count), count)]
+    symbol_of(materials, pixels, (high_table, low_table), fetched, mine)
+    pl.semaphore_wait(barrier, devices - 1)
+    sent = []
+    for i in range(1, devices):
+        copy = pltpu.make_async_remote_copy(
+            src_ref=mine,
+            dst_ref=mine,
+            send_sem=send_sem.at[i],
+            recv_sem=recv_sem.at[i],
+            device_id={"long": lax.rem(me + i, devices)},
+        )
+        copy.start()
+        sent.append(copy)
+
+    columns, y_orders, _, orders = panel.shape
+    lines = symbol.shape[0]
+    kept = min(y_orders, lines)
+    padded = spread_high.shape[1] // 2
+    folded[...] = jnp.zeros(folded.shape, jnp.float32)
+    for c in range(columns):
+        for part in range(2):
+            base = part * padded
+            folded[c, base : base + kept, :orders] = panel[c, :kept, part, :]
+            for first in range(kept, y_orders, kept):
+                size = min(kept, y_orders - first)
+                folded[c, base : base + size, :orders] += panel[c, first : first + size, part, :]
+        high, low = split(folded[c])
+        value = (
+            mul(spread_high[...], high) + mul(spread_high[...], low) + mul(spread_low[...], high)
+        )
+        rows = slice(c * 2 * lines, (c + 1) * 2 * lines)
+        spread[rows, :] = value
+        high, low = split(value)
+        start[rows, :] = mul_table(high, low, forward_high[...], forward_low[...])
+
+    for copy in sent:
+        copy.wait()
+    symbol[...] = landed[...]
 
 
 def panel_kernel(
     materials,
-    panel,
     symbol,
-    spread_high,
-    spread_low,
+    spread,
+    start,
     gather_high,
     gather_low,
-    forward_high,
-    forward_low,
     backward_high,
     backward_low,
     even_high,
@@ -127,14 +210,11 @@
     odd_high,
     odd_low,
     out,
-    folded,
-    spread,
-    start,
     state,
     high_side,
     low_side,
 ):
-    columns, _, y_orders, orders = panel.shape
+    columns, y_orders, _, orders = out.shape
     lines, width = symbol.shape
     lanes = width // 2
     blocks = lines // BLOCK
@@ -142,29 +222,9 @@
     units = columns * blocks
     group = 2 if units % 2 == 0 else 1
     kept = min(y_orders, lines)
-    padded = spread_high.shape[1] // 2
-
-    folded[...] = jnp.zeros(folded.shape, jnp.float32)
-    for c in range(columns):
-        for part in range(2):
-            base = part * padded
-            folded[c, base : base + kept, :orders] = panel[c, part, :kept, :]
-            for first in range(kept, y_orders, kept):
-                size = min(kept, y_orders - first)
-                folded[c, base : base + size, :orders] += panel[c, part, first : first + size, :]
-        high, low = split(folded[c])
-        spread[c * 2 * lines : (c + 1) * 2 * lines, :] = (
-            mul(spread_high[...], high) + mul(spread_high[...], low) + mul(spread_low[...], high)
-        )
-
-    for g in range(0, units, group):
-        rows = slice(g * unit, (g + group) * unit)
-        high, low = split(spread[rows, :])
-        value = mul_table(high, low, forward_high[...], forward_low[...])
-        start[rows, :] = value
-        state[rows, :] = value
-
-    def weigh(u):
+    padded = gather_high.shape[0] // 2
+
+    def weigh(u, state):
         real = slice(u * unit, u * unit + BLOCK)
         imag = slice(u * unit + BLOCK, (u + 1) * unit)
         here = slice((u % blocks) * BLOCK, (u % blocks + 1) * BLOCK)
@@ -184,33 +244,38 @@
             high_side[rows, cols] = high
             low_side[rows, cols] = low
 
-    def sweep(_, carry):
+    def sweep(source):
         for g in range(0, units, group):
             rows = slice(g * unit, (g + group) * unit)
             for u in range(g, g + group):
-                weigh(u)
+                weigh(u, source)
             state[rows, :lanes] = start[rows, :lanes] + mul_table(
                 high_side[rows, :lanes], low_side[rows, :lanes], even_high[...], even_low[...]
             )
             state[rows, lanes:] = start[rows, lanes:] + mul_table(
                 high_side[rows, lanes:], low_side[rows, lanes:], odd_high[...], odd_low[...]
             )
+
+    sweep(start)
+
+    def again(_, carry):
+        sweep(state)
         return carry
 
-    lax.fori_loop(0, 2**NS_ITERS - 2, sweep, 0)
+    lax.fori_loop(0, 2**NS_ITERS - 3, again, 0)
 
     scale = scale_of(materials, (1, lanes))
     for g in range(0, units, group):
         rows = slice(g * unit, (g + group) * unit)
         for u in range(g, g + group):
-            weigh(u)
-        spread[rows, :] = scale * (
+            weigh(u, state)
+        state[rows, :lanes] = scale * (
             spread[rows, :]
             + mul_table(high_side[rows, :], low_side[rows, :], backward_high[...], backward_low[...])
         )
 
     for c in range(columns):
-        high, low = split(spread[c * 2 * lines : (c + 1) * 2 * lines, :])
+        high, low = split(state[c * 2 * lines : (c + 1) * 2 * lines, :lanes])
         value = (
             mul(gather_high[...], high) + mul(gather_high[...], low) + mul(gather_low[...], high)
         )
@@ -218,7 +283,7 @@
             base = part * padded
             for first in range(0, y_orders, kept):
                 size = min(kept, y_orders - first)
-                out[c, part, first : first + size, :] = value[base : base + size, :orders]
+                out[c, first : first + size, part, :] = value[base : base + size, :orders]
 
 
 def whole(count):
@@ -228,41 +293,55 @@
 def local(pixel_map, materials, mode_panel):
     rows, pixels = pixel_map.shape
     columns, _, y_orders, orders = mode_panel.shape
-    lines = rows * lax.axis_size("long")
+    devices = lax.axis_size("long")
+    lines = rows * devices
     lanes = round_up(orders, 2 * BLOCK)
     width = 2 * lanes
+    total = columns * 2 * lines
     scalars = pl.BlockSpec(memory_space=pltpu.SMEM)
-    params = pltpu.CompilerParams(vmem_limit_bytes=VMEM_BYTES)
-    symbol = pl.pallas_call(
-        symbol_kernel,
-        out_shape=jax.ShapeDtypeStruct((rows, width), jnp.float32),
-        in_specs=[scalars] + whole(3),
-        out_specs=pl.BlockSpec(memory_space=pltpu.VMEM),
-        compiler_params=params,
-        name="symbol",
-    )(materials, pixel_map, *map(jnp.asarray, symbol_table(orders, pixels)))
-    symbol = lax.all_gather(symbol, "long", axis=0, tiled=True)
-    spread_table, gather_table = line_tables(y_orders, lines)
+    symbol_pair = symbol_table(orders, pixels)
+    spread_pair, gather_pair = line_tables(y_orders, lines)
     forward, backward, even, odd = order_tables(orders)
-    tables = [*spread_table, *gather_table, *forward, *backward, *even, *odd]
-    total = columns * 2 * lines
-    folded_rows = spread_table[0].shape[1]
-    return pl.pallas_call(
+    tables = [*spread_pair, *forward]
+    panel = mode_panel.transpose(0, 2, 1, 3)
+    symbol, spread, start = pl.pallas_call(
+        gather_kernel,
+        out_shape=[
+            jax.ShapeDtypeStruct((lines, width), jnp.float32),
+            jax.ShapeDtypeStruct((total, lanes), jnp.float32),
+            jax.ShapeDtypeStruct((total, width), jnp.float32),
+        ],
+        in_specs=[scalars] + whole(2 + len(tables)) + [pl.BlockSpec(memory_space=pl.ANY)] * 2,
+        out_specs=whole(3),
+        scratch_shapes=[
+            pltpu.VMEM((pixels, width), jnp.bfloat16),
+            pltpu.VMEM((pixels, width), jnp.bfloat16),
+            pltpu.VMEM((lines, width), jnp.float32),
+            pltpu.VMEM((columns, spread_pair[0].shape[1], lanes), jnp.float32),
+            pltpu.SemaphoreType.DMA((2 * CHUNKS,)),
+            pltpu.SemaphoreType.DMA((devices,)),
+            pltpu.SemaphoreType.DMA((devices,)),
+        ],
+        compiler_params=pltpu.CompilerParams(
+            vmem_limit_bytes=VMEM_BYTES, collective_id=0, has_side_effects=True
+        ),
+        name="gather",
+    )(materials, pixel_map, panel, *map(jnp.asarray, tables), *map(jnp.asarray, symbol_pair))
+    tables = [*gather_pair, *backward, *even, *odd]
+    result = pl.pallas_call(
         panel_kernel,
-        out_shape=jax.ShapeDtypeStruct(mode_panel.shape, jnp.float32),
-        in_specs=[scalars] + whole(2 + len(tables)),
+        out_shape=jax.ShapeDtypeStruct(panel.shape, jnp.float32),
+        in_specs=[scalars] + whole(3 + len(tables)),
         out_specs=pl.BlockSpec(memory_space=pltpu.VMEM),
         scratch_shapes=[
-            pltpu.VMEM((columns, folded_rows, lanes), jnp.float32),
-            pltpu.VMEM((total, lanes), jnp.float32),
-            pltpu.VMEM((total, width), jnp.float32),
             pltpu.VMEM((total, width), jnp.float32),
             pltpu.VMEM((total, width), jnp.bfloat16),
             pltpu.VMEM((total, width), jnp.bfloat16),
         ],
-        compiler_params=params,
+        compiler_params=pltpu.CompilerParams(vmem_limit_bytes=VMEM_BYTES),
         name="panel",
-    )(materials, mode_panel, symbol, *map(jnp.asarray, tables))
+    )(materials, symbol, spread, start, *map(jnp.asarray, tables))
+    return result.transpose(0, 2, 1, 3)
 
 
 def solution(mesh):

time: 47.6 us -> 33.2 us (0.70)
  blocking collectives: 25.3 us -> 0 us
  Pallas kernels: 16.7 us -> 22.9 us
  local copies, waits for them, and re-layouts: 5.25 us -> 9.86 us
    all_gather x1 -> x0, blocking collectives: 25.3 us -> none  [local(): symbol = lax.all_gather(symbol, 'long', axis=0, tiled=True)]
    unnamed x3 -> x34, local copies, waits for them, and re-layouts: 1.36 us -> 9.86 us
    pallas_call x2, Pallas kernels: 16.7 us -> 22.9 us  [the longest x1 11.9 us: local(): pl.pallas_call(gather_kernel, out_shape=[jax.ShapeDtypeStruct((lines, wid...]
    pallas_call x1 -> x0, local copies, waits for them, and re-layouts: 3.89 us -> none  [local(): pl.pallas_call(panel_kernel, out_shape=jax.ShapeDtypeStruct(mode_panel.sh...]
where the time goes in v1:
time: 33.2 us; the launch traced here: 32.8 us
  Pallas kernels  22.9 us (69%)
  local copies, waits for them, and re-layouts  9.86 us (30%)
    pallas_call x1, Pallas kernels, local(): pl.pallas_call(gather_kernel, out_shape=[jax.ShapeDtypeStruct((lines, wid...  11.9 us
    pallas_call x1, Pallas kernels, local(): pl.pallas_call(panel_kernel, out_shape=jax.ShapeDtypeStruct(panel.shape,...  11 us
    unnamed x34, local copies, waits for them, and re-layouts  9.86 us

profile of v1, /device:TPU:1, one launch (start us, length us, event | category | flops | bytes accessed | tf_op | source)
XLA Modules:
  0.0 32.8 jit_solution(6672456539262213515)
XLA Ops:
  0.0 0.0 copy-start
  0.0 1.6 %copy-done = bf16[2048,512]{1,0:T(8,128)(2,1)S(1)} copy-done((bf16[2048,512]{1,0:T(8,128)(2,1)S(1)}, bf16[2048,512]{1,0:T(8,128)(2,1)}, u32[]{:S(2)}) %copy-start) | copy-done | bytes 2097176
  1.6 1.6 %copy-done.1 = bf16[2048,512]{1,0:T(8,128)(2,1)S(1)} copy-done((bf16[2048,512]{1,0:T(8,128)(2,1)S(1)}, bf16[2048,512]{1,0:T(8,128)(2,1)}, u32[]{:S(2)}) %copy-start.1) | copy-done | bytes 2097176
  3.2 1.4 %copy-done.2 = f32[4,2,201,201]{3,1,2,0:T(2,128)S(1)} copy-done((f32[4,2,201,201]{3,1,2,0:T(2,128)S(1)}, f32[4,2,201,201]{3,1,2,0:T(2,128)}, u32[]{:S(2)}) %copy-start.2) | copy-done | bytes 1292856
  4.6 0.9 %copy-done.5 = bf16[256,512]{1,0:T(8,128)(2,1)S(1)} copy-done((bf16[256,512]{1,0:T(8,128)(2,1)S(1)}, bf16[256,512]{1,0:T(8,128)(2,1)}, u32[]{:S(2)}) %copy-start.5) | copy-done | bytes 262168
  5.6 0.9 %copy-done.6 = bf16[256,512]{1,0:T(8,128)(2,1)S(1)} copy-done((bf16[256,512]{1,0:T(8,128)(2,1)S(1)}, bf16[256,512]{1,0:T(8,128)(2,1)}, u32[]{:S(2)}) %copy-start.6) | copy-done | bytes 262168
  6.5 0.9 %copy-done.13 = bf16[256,256]{1,0:T(8,128)(2,1)S(1)} copy-done((bf16[256,256]{1,0:T(8,128)(2,1)S(1)}, bf16[256,256]{1,0:T(8,128)(2,1)}, u32[]{:S(2)}) %copy-start.13) | copy-done | bytes 131096
  7.4 0.9 %copy-done.14 = bf16[256,256]{1,0:T(8,128)(2,1)S(1)} copy-done((bf16[256,256]{1,0:T(8,128)(2,1)S(1)}, bf16[256,256]{1,0:T(8,128)(2,1)}, u32[]{:S(2)}) %copy-start.14) | copy-done | bytes 131096
  8.3 0.8 %copy-done.15 = s32[8,2048]{1,0:T(8,128)S(1)} copy-done((s32[8,2048]{1,0:T(8,128)S(1)}, s32[8,2048]{1,0:T(8,128)}, u32[]{:S(2)}) %copy-start.15) | copy-done | bytes 65560
  9.2 0.7 %copy-done.16 = f32[4]{0:T(128)S(1)} copy-done((f32[4]{0:T(128)S(1)}, f32[4]{0:T(128)}, u32[]{:S(2)}) %copy-start.16) | copy-done | bytes 40
  9.8 0.0 copy-start.9
  9.8 0.0 copy-start.10
  9.9 0.0 copy-start.11
  9.9 0.0 copy-start.12
  9.9 11.9 %gather.1 = (f32[128,512]{1,0:T(8,128)S(1)}, f32[1024,256]{1,0:T(8,128)S(1)}, f32[1024,512]{1,0:T(8,128)S(1)}) custom-call(f32[4]{0:T(128)S(1)} %copy-done.16, s32[8,2048]{1,0:T(8,128)S(1)} %copy-done.15, f32[4,201,2,201]{3,2,1,0:T(2,128)S(1)} %bitcast.2, bf16[256,256]{1,0:T(8,128)(2,1)S(1)} %copy-done.14, bf16[256,256]{1,0:T(8,128)(2,1)S(1)} %copy-done.13, ...), custom_call_target="tpu_custom_call" | custom-call | tf_op jit(solution)/shard_map/gather/pallas_call | solution.py:307
  21.8 0.0 copy-done.3
  21.8 0.0 copy-done.4
  21.8 0.0 copy-done.7
  21.8 0.0 copy-done.8
  21.8 0.0 copy-done.9
  21.8 0.0 copy-done.10
  21.8 0.0 copy-done.11
  21.8 0.0 copy-done.12
  21.8 11.0 %panel.1 = f32[4,201,2,201]{3,2,1,0:T(2,128)} custom-call(f32[4]{0:T(128)S(1)} %copy-done.16, f32[128,512]{1,0:T(8,128)S(1)} %get-tuple-element.8.symbol, f32[1024,256]{1,0:T(8,128)S(1)} %get-tuple-element.9.spread, f32[1024,512]{1,0:T(8,128)S(1)} %get-tuple-element.10.start, bf16[256,256]{1,0:T(8,128)(2,1)S(1)} %copy-done.12, ...), custom_call_target="tpu_custom_call" | custom-call | tf_op jit(solution)/shard_map/panel/pallas_call | solution.py:331
  (12 shorter events, 0.0 us)
Async XLA Ops:
  0.0 1.6 %copy-start = (bf16[2048,512]{1,0:T(8,128)(2,1)S(1)}, bf16[2048,512]{1,0:T(8,128)(2,1)}, u32[]{:S(2)}) copy-start(bf16[2048,512]{1,0:T(8,128)(2,1)} %constant.33.clone.table_low) | copy-start | bytes 6291460
  1.6 1.6 %copy-start.1 = (bf16[2048,512]{1,0:T(8,128)(2,1)S(1)}, bf16[2048,512]{1,0:T(8,128)(2,1)}, u32[]{:S(2)}) copy-start(bf16[2048,512]{1,0:T(8,128)(2,1)} %constant.32.clone.table_high) | copy-start | bytes 6291460
  3.2 1.4 %copy-start.2 = (f32[4,2,201,201]{3,1,2,0:T(2,128)S(1)}, f32[4,2,201,201]{3,1,2,0:T(2,128)}, u32[]{:S(2)}) copy-start(f32[4,2,201,201]{3,1,2,0:T(2,128)} %param.19) | copy-start | bytes 3878500
  4.6 0.9 %copy-start.5 = (bf16[256,512]{1,0:T(8,128)(2,1)S(1)}, bf16[256,512]{1,0:T(8,128)(2,1)}, u32[]{:S(2)}) copy-start(bf16[256,512]{1,0:T(8,128)(2,1)} %constant.31.clone.forward_low) | copy-start | bytes 786436
  5.6 0.9 %copy-start.6 = (bf16[256,512]{1,0:T(8,128)(2,1)S(1)}, bf16[256,512]{1,0:T(8,128)(2,1)}, u32[]{:S(2)}) copy-start(bf16[256,512]{1,0:T(8,128)(2,1)} %constant.30.clone.forward_high) | copy-start | bytes 786436
  6.5 0.9 %copy-start.13 = (bf16[256,256]{1,0:T(8,128)(2,1)S(1)}, bf16[256,256]{1,0:T(8,128)(2,1)}, u32[]{:S(2)}) copy-start(bf16[256,256]{1,0:T(8,128)(2,1)} %constant.29.clone.spread_low) | copy-start | bytes 393220
  7.4 0.9 %copy-start.14 = (bf16[256,256]{1,0:T(8,128)(2,1)S(1)}, bf16[256,256]{1,0:T(8,128)(2,1)}, u32[]{:S(2)}) copy-start(bf16[256,256]{1,0:T(8,128)(2,1)} %constant.28.clone.spread_high) | copy-start | bytes 393220
  8.3 0.8 %copy-start.15 = (s32[8,2048]{1,0:T(8,128)S(1)}, s32[8,2048]{1,0:T(8,128)}, u32[]{:S(2)}) copy-start(s32[8,2048]{1,0:T(8,128)} %pixel_rows.1) | copy-start | bytes 196612
  9.2 0.7 %copy-start.16 = (f32[4]{0:T(128)S(1)}, f32[4]{0:T(128)}, u32[]{:S(2)}) copy-start(f32[4]{0:T(128)} %materials.3) | copy-start | bytes 52
  9.8 11.9 %copy-start.3 = (bf16[512,256]{1,0:T(8,128)(2,1)S(1)}, bf16[512,256]{1,0:T(8,128)(2,1)}, u32[]{:S(2)}) copy-start(bf16[512,256]{1,0:T(8,128)(2,1)} %constant.37.clone.backward_low) | copy-start | bytes 786436
  9.8 12.0 %copy-start.4 = (bf16[512,256]{1,0:T(8,128)(2,1)S(1)}, bf16[512,256]{1,0:T(8,128)(2,1)}, u32[]{:S(2)}) copy-start(bf16[512,256]{1,0:T(8,128)(2,1)} %constant.36.clone.backward_high) | copy-start | bytes 786436
  9.8 12.0 %copy-start.7 = (bf16[256,256]{1,0:T(8,128)(2,1)S(1)}, bf16[256,256]{1,0:T(8,128)(2,1)}, u32[]{:S(2)}) copy-start(bf16[256,256]{1,0:T(8,128)(2,1)} %constant.41.clone.odd_low) | copy-start | bytes 393220
  9.8 12.0 %copy-start.8 = (bf16[256,256]{1,0:T(8,128)(2,1)S(1)}, bf16[256,256]{1,0:T(8,128)(2,1)}, u32[]{:S(2)}) copy-start(bf16[256,256]{1,0:T(8,128)(2,1)} %constant.40.clone.odd_high) | copy-start | bytes 393220
  9.8 12.0 %copy-start.9 = (bf16[256,256]{1,0:T(8,128)(2,1)S(1)}, bf16[256,256]{1,0:T(8,128)(2,1)}, u32[]{:S(2)}) copy-start(bf16[256,256]{1,0:T(8,128)(2,1)} %constant.39.clone.even_low) | copy-start | bytes 393220
  9.8 12.0 %copy-start.10 = (bf16[256,256]{1,0:T(8,128)(2,1)S(1)}, bf16[256,256]{1,0:T(8,128)(2,1)}, u32[]{:S(2)}) copy-start(bf16[256,256]{1,0:T(8,128)(2,1)} %constant.38.clone.even_high) | copy-start | bytes 393220
  9.9 12.0 %copy-start.11 = (bf16[256,256]{1,0:T(8,128)(2,1)S(1)}, bf16[256,256]{1,0:T(8,128)(2,1)}, u32[]{:S(2)}) copy-start(bf16[256,256]{1,0:T(8,128)(2,1)} %constant.35.clone.gather_low) | copy-start | bytes 393220
  9.9 12.0 %copy-start.12 = (bf16[256,256]{1,0:T(8,128)(2,1)S(1)}, bf16[256,256]{1,0:T(8,128)(2,1)}, u32[]{:S(2)}) copy-start(bf16[256,256]{1,0:T(8,128)(2,1)} %constant.34.clone.gather_high) | copy-start | bytes 393220

commit v2 on v1

--- a/solution.py
+++ b/solution.py
@@ -12,7 +12,7 @@
 NS_ITERS = 3
 BLOCK = 128
 CHUNKS = 4
-VMEM_BYTES = 28 * 1024 * 1024
+VMEM_BYTES = 62 * 1024 * 1024
 
 
 def round_up(value, step):
@@ -116,7 +116,7 @@
     sums[:, lanes:] = -scaled[:, lanes:]
 
 
-def gather_kernel(
+def apply_kernel(
     materials,
     pixel_rows,
     panel,
@@ -124,25 +124,76 @@
     spread_low,
     forward_high,
     forward_low,
+    gather_high_far,
+    gather_low_far,
+    backward_high_far,
+    backward_low_far,
+    even_high_far,
+    even_low_far,
+    odd_high_far,
+    odd_low_far,
     table_high,
     table_low,
-    symbol,
-    spread,
-    start,
+    out,
+    scalars,
+    pixels,
+    panel_here,
+    spread_high_here,
+    spread_low_here,
+    forward_high_here,
+    forward_low_here,
+    gather_high,
+    gather_low,
+    backward_high,
+    backward_low,
+    even_high,
+    even_low,
+    odd_high,
+    odd_low,
     high_table,
     low_table,
     landed,
     folded,
+    spread,
+    start,
+    state,
+    high_side,
+    low_side,
+    result,
     fetch_sem,
     send_sem,
     recv_sem,
+    store_sem,
 ):
+    sources = (
+        (materials, scalars),
+        (pixel_rows, pixels),
+        (panel, panel_here),
+        (spread_high, spread_high_here),
+        (spread_low, spread_low_here),
+        (forward_high, forward_high_here),
+        (forward_low, forward_low_here),
+        (gather_high_far, gather_high),
+        (gather_low_far, gather_low),
+        (backward_high_far, backward_high),
+        (backward_low_far, backward_low),
+        (even_high_far, even_high),
+        (even_low_far, even_low),
+        (odd_high_far, odd_high),
+        (odd_low_far, odd_low),
+    )
+    fetches = [
+        pltpu.make_async_copy(source, target, fetch_sem.at[2 * CHUNKS + i])
+        for i, (source, target) in enumerate(sources)
+    ]
+    early, late = fetches[:7], fetches[7:]
+    for copy in early[:2]:
+        copy.start()
     me = lax.axis_index("long")
     devices = lax.axis_size("long")
     barrier = pltpu.get_barrier_semaphore()
     for i in range(1, devices):
         pl.semaphore_signal(barrier, inc=1, device_id={"long": lax.rem(me + i, devices)})
-    pixels = pixel_rows[...]
     depth = table_high.shape[0] // CHUNKS
     fetched = []
     for i in range(CHUNKS):
@@ -154,9 +205,13 @@
         for copy in copies:
             copy.start()
         fetched.append(copies)
+    for copy in early[2:] + late:
+        copy.start()
     count = pixels.shape[0]
     mine = landed.at[pl.ds(pl.multiple_of(me * count, count), count)]
-    symbol_of(materials, pixels, (high_table, low_table), fetched, mine)
+    for copy in early[:2]:
+        copy.wait()
+    symbol_of(scalars, pixels[...], (high_table, low_table), fetched, mine)
     pl.semaphore_wait(barrier, devices - 1)
     sent = []
     for i in range(1, devices):
@@ -171,51 +226,37 @@
         sent.append(copy)
 
     columns, y_orders, _, orders = panel.shape
-    lines = symbol.shape[0]
+    lines = landed.shape[0]
     kept = min(y_orders, lines)
     padded = spread_high.shape[1] // 2
     folded[...] = jnp.zeros(folded.shape, jnp.float32)
+    for copy in early[2:]:
+        copy.wait()
     for c in range(columns):
         for part in range(2):
             base = part * padded
-            folded[c, base : base + kept, :orders] = panel[c, :kept, part, :]
+            folded[c, base : base + kept, :orders] = panel_here[c, :kept, part, :]
             for first in range(kept, y_orders, kept):
                 size = min(kept, y_orders - first)
-                folded[c, base : base + size, :orders] += panel[c, first : first + size, part, :]
+                folded[c, base : base + size, :orders] += panel_here[c, first : first + size, part, :]
         high, low = split(folded[c])
         value = (
-            mul(spread_high[...], high) + mul(spread_high[...], low) + mul(spread_low[...], high)
+            mul(spread_high_here[...], high)
+            + mul(spread_high_here[...], low)
+            + mul(spread_low_here[...], high)
         )
         rows = slice(c * 2 * lines, (c + 1) * 2 * lines)
         spread[rows, :] = value
         high, low = split(value)
-        start[rows, :] = mul_table(high, low, forward_high[...], forward_low[...])
+        start[rows, :] = mul_table(high, low, forward_high_here[...], forward_low_here[...])
 
     for copy in sent:
         copy.wait()
-    symbol[...] = landed[...]
-
-
-def panel_kernel(
-    materials,
-    symbol,
-    spread,
-    start,
-    gather_high,
-    gather_low,
-    backward_high,
-    backward_low,
-    even_high,
-    even_low,
-    odd_high,
-    odd_low,
-    out,
-    state,
-    high_side,
-    low_side,
-):
-    columns, y_orders, _, orders = out.shape
-    lines, width = symbol.shape
+    symbol = landed
+    for copy in late:
+        copy.wait()
+
+    width = symbol.shape[1]
     lanes = width // 2
     blocks = lines // BLOCK
     unit = 2 * BLOCK
@@ -256,15 +297,10 @@
                 high_side[rows, lanes:], low_side[rows, lanes:], odd_high[...], odd_low[...]
             )
 
-    sweep(start)
-
-    def again(_, carry):
-        sweep(state)
-        return carry
-
-    lax.fori_loop(0, 2**NS_ITERS - 3, again, 0)
-
-    scale = scale_of(materials, (1, lanes))
+    for i in range(2**NS_ITERS - 2):
+        sweep(state if i else start)
+
+    scale = scale_of(scalars, (1, lanes))
     for g in range(0, units, group):
         rows = slice(g * unit, (g + group) * unit)
         for u in range(g, g + group):
@@ -274,6 +310,7 @@
             + mul_table(high_side[rows, :], low_side[rows, :], backward_high[...], backward_low[...])
         )
 
+    stores = []
     for c in range(columns):
         high, low = split(state[c * 2 * lines : (c + 1) * 2 * lines, :lanes])
         value = (
@@ -283,11 +320,11 @@
             base = part * padded
             for first in range(0, y_orders, kept):
                 size = min(kept, y_orders - first)
-                out[c, first : first + size, part, :] = value[base : base + size, :orders]
-
-
-def whole(count):
-    return [pl.BlockSpec(memory_space=pltpu.VMEM)] * count
+                result[c, first : first + size, part, :] = value[base : base + size, :orders]
+        stores.append(pltpu.make_async_copy(result.at[c], out.at[c], store_sem.at[c]))
+        stores[-1].start()
+    for store in stores:
+        store.wait()
 
 
 def local(pixel_map, materials, mode_panel):
@@ -298,49 +335,41 @@
     lanes = round_up(orders, 2 * BLOCK)
     width = 2 * lanes
     total = columns * 2 * lines
-    scalars = pl.BlockSpec(memory_space=pltpu.SMEM)
     symbol_pair = symbol_table(orders, pixels)
     spread_pair, gather_pair = line_tables(y_orders, lines)
     forward, backward, even, odd = order_tables(orders)
-    tables = [*spread_pair, *forward]
+    tables = [*spread_pair, *forward, *gather_pair, *backward, *even, *odd]
     panel = mode_panel.transpose(0, 2, 1, 3)
-    symbol, spread, start = pl.pallas_call(
-        gather_kernel,
-        out_shape=[
-            jax.ShapeDtypeStruct((lines, width), jnp.float32),
-            jax.ShapeDtypeStruct((total, lanes), jnp.float32),
-            jax.ShapeDtypeStruct((total, width), jnp.float32),
-        ],
-        in_specs=[scalars] + whole(2 + len(tables)) + [pl.BlockSpec(memory_space=pl.ANY)] * 2,
-        out_specs=whole(3),
+    result = pl.pallas_call(
+        apply_kernel,
+        out_shape=jax.ShapeDtypeStruct(panel.shape, jnp.float32),
+        in_specs=[pl.BlockSpec(memory_space=pl.ANY)] * (5 + len(tables)),
+        out_specs=pl.BlockSpec(memory_space=pl.ANY),
         scratch_shapes=[
+            pltpu.SMEM(materials.shape, jnp.float32),
+            pltpu.VMEM(pixel_map.shape, jnp.int32),
+            pltpu.VMEM(panel.shape, jnp.float32),
+            *[pltpu.VMEM(table.shape, jnp.bfloat16) for table in tables],
             pltpu.VMEM((pixels, width), jnp.bfloat16),
             pltpu.VMEM((pixels, width), jnp.bfloat16),
             pltpu.VMEM((lines, width), jnp.float32),
             pltpu.VMEM((columns, spread_pair[0].shape[1], lanes), jnp.float32),
-            pltpu.SemaphoreType.DMA((2 * CHUNKS,)),
+            pltpu.VMEM((total, lanes), jnp.float32),
+            pltpu.VMEM((total, width), jnp.float32),
+            pltpu.VMEM((total, width), jnp.float32),
+            pltpu.VMEM((total, width), jnp.bfloat16),
+            pltpu.VMEM((total, width), jnp.bfloat16),
+            pltpu.VMEM(panel.shape, jnp.float32),
+            pltpu.SemaphoreType.DMA((2 * CHUNKS + 3 + len(tables),)),
             pltpu.SemaphoreType.DMA((devices,)),
             pltpu.SemaphoreType.DMA((devices,)),
+            pltpu.SemaphoreType.DMA((columns,)),
         ],
         compiler_params=pltpu.CompilerParams(
             vmem_limit_bytes=VMEM_BYTES, collective_id=0, has_side_effects=True
         ),
-        name="gather",
+        name="apply",
     )(materials, pixel_map, panel, *map(jnp.asarray, tables), *map(jnp.asarray, symbol_pair))
-    tables = [*gather_pair, *backward, *even, *odd]
-    result = pl.pallas_call(
-        panel_kernel,
-        out_shape=jax.ShapeDtypeStruct(panel.shape, jnp.float32),
-        in_specs=[scalars] + whole(3 + len(tables)),
-        out_specs=pl.BlockSpec(memory_space=pltpu.VMEM),
-        scratch_shapes=[
-            pltpu.VMEM((total, width), jnp.float32),
-            pltpu.VMEM((total, width), jnp.bfloat16),
-            pltpu.VMEM((total, width), jnp.bfloat16),
-        ],
-        compiler_params=pltpu.CompilerParams(vmem_limit_bytes=VMEM_BYTES),
-        name="panel",
-    )(materials, symbol, spread, start, *map(jnp.asarray, tables))
     return result.transpose(0, 2, 1, 3)
 
 

time: 33.2 us -> 23.8 us (0.72)
  local copies, waits for them, and re-layouts: 9.86 us -> 3.17 us
  Pallas kernels: 22.9 us -> 20.5 us
    unnamed x34 -> x1, local copies, waits for them, and re-layouts: 9.86 us -> 3.17 us
    pallas_call x2 -> x1, Pallas kernels: 22.9 us -> 20.5 us  [local(): pl.pallas_call(apply_kernel, out_shape=jax.ShapeDtypeStruct(panel.shape,...]
where the time goes in v2:
time: 23.8 us; the launch traced here: 23.6 us
  Pallas kernels  20.5 us (86%)
  local copies, waits for them, and re-layouts  3.17 us (13%)
    pallas_call x1, Pallas kernels, local(): pl.pallas_call(apply_kernel, out_shape=jax.ShapeDtypeStruct(panel.shape,...  20.5 us
    unnamed x1, local copies, waits for them, and re-layouts  3.17 us

profile of v2, /device:TPU:1, one launch (start us, length us, event | category | flops | bytes accessed | tf_op | source)
XLA Modules:
  0.0 23.6 jit_solution(10867687331417942845)
XLA Ops:
  0.0 20.5 %apply.1 = f32[4,201,2,201]{3,2,1,0:T(2,128)} custom-call(f32[4]{0:T(128)} %materials.1, s32[8,2048]{1,0:T(8,128)} %pixel_rows.1, f32[4,201,2,201]{3,2,1,0:T(2,128)} %bitcast.3, bf16[256,256]{1,0:T(8,128)(2,1)} %constant.28.clone.spread_high, bf16[256,256]{1,0:T(8,128)(2,1)} %constant.29.clone.spread_low, bf16[256,512]{1,0:T(8,128)(2,1)} %constant.30.clone.forward_high, ...), custom_call_target="tpu_custom_call" | custom-call | tf_op jit(solution)/shard_map/apply/pallas_call | solution.py:343
  20.5 3.2 %copy.19 = f32[4,2,201,201]{3,1,2,0:T(2,128)} copy(f32[4,2,201,201]{3,1,2,0:T(2,128)} %bitcast.2) | data formatting | bytes 2585664

commit v3 on v2

--- a/solution.py
+++ b/solution.py
@@ -124,8 +124,6 @@
     spread_low,
     forward_high,
     forward_low,
-    gather_high_far,
-    gather_low_far,
     backward_high_far,
     backward_low_far,
     even_high_far,
@@ -142,8 +140,6 @@
     spread_low_here,
     forward_high_here,
     forward_low_here,
-    gather_high,
-    gather_low,
     backward_high,
     backward_low,
     even_high,
@@ -159,7 +155,6 @@
     state,
     high_side,
     low_side,
-    result,
     fetch_sem,
     send_sem,
     recv_sem,
@@ -173,8 +168,6 @@
         (spread_low, spread_low_here),
         (forward_high, forward_high_here),
         (forward_low, forward_low_here),
-        (gather_high_far, gather_high),
-        (gather_low_far, gather_low),
         (backward_high_far, backward_high),
         (backward_low_far, backward_low),
         (even_high_far, even_high),
@@ -191,9 +184,18 @@
         copy.start()
     me = lax.axis_index("long")
     devices = lax.axis_size("long")
+    cores = 2
+    chips = devices // cores
+    chip = me // cores
+    core = lax.rem(me, cores)
+    sibling = chip * cores + (1 - core)
+
+    def twin(i):
+        return lax.rem(chip + i, chips) * cores + core
+
     barrier = pltpu.get_barrier_semaphore()
-    for i in range(1, devices):
-        pl.semaphore_signal(barrier, inc=1, device_id={"long": lax.rem(me + i, devices)})
+    for peer in [sibling] + [twin(i) for i in range(1, chips)]:
+        pl.semaphore_signal(barrier, inc=1, device_id={"long": peer})
     depth = table_high.shape[0] // CHUNKS
     fetched = []
     for i in range(CHUNKS):
@@ -208,22 +210,34 @@
     for copy in early[2:] + late:
         copy.start()
     count = pixels.shape[0]
-    mine = landed.at[pl.ds(pl.multiple_of(me * count, count), count)]
+
+    def slot(device):
+        return landed.at[pl.ds(pl.multiple_of(device * count, count), count)]
+
+    def send(device, peer, i):
+        return pltpu.make_async_remote_copy(
+            src_ref=slot(device),
+            dst_ref=slot(device),
+            send_sem=send_sem.at[i],
+            recv_sem=recv_sem.at[i],
+            device_id={"long": peer},
+        )
+
+    mine = slot(me)
     for copy in early[:2]:
         copy.wait()
     symbol_of(scalars, pixels[...], (high_table, low_table), fetched, mine)
-    pl.semaphore_wait(barrier, devices - 1)
-    sent = []
-    for i in range(1, devices):
-        copy = pltpu.make_async_remote_copy(
-            src_ref=mine,
-            dst_ref=mine,
-            send_sem=send_sem.at[i],
-            recv_sem=recv_sem.at[i],
-            device_id={"long": lax.rem(me + i, devices)},
-        )
+    pl.semaphore_wait(barrier, chips)
+    sent = [send(me, twin(i), i) for i in range(1, chips)]
+    handed = [send(me, sibling, chips)]
+    for copy in sent[::-1] + handed:
         copy.start()
-        sent.append(copy)
+
+    def hand_on():
+        for i in range(1, chips):
+            sent[i - 1].wait()
+            handed.append(send(twin(chips - i), sibling, chips + i))
+            handed[-1].start()
 
     columns, y_orders, _, orders = panel.shape
     lines = landed.shape[0]
@@ -249,8 +263,10 @@
         spread[rows, :] = value
         high, low = split(value)
         start[rows, :] = mul_table(high, low, forward_high_here[...], forward_low_here[...])
-
-    for copy in sent:
+        if c == max(columns - 2, 0):
+            hand_on()
+
+    for copy in handed:
         copy.wait()
     symbol = landed
     for copy in late:
@@ -262,8 +278,6 @@
     unit = 2 * BLOCK
     units = columns * blocks
     group = 2 if units % 2 == 0 else 1
-    kept = min(y_orders, lines)
-    padded = gather_high.shape[0] // 2
 
     def weigh(u, state):
         real = slice(u * unit, u * unit + BLOCK)
@@ -301,18 +315,55 @@
         sweep(state if i else start)
 
     scale = scale_of(scalars, (1, lanes))
+    stores = []
     for g in range(0, units, group):
         rows = slice(g * unit, (g + group) * unit)
         for u in range(g, g + group):
             weigh(u, state)
-        state[rows, :lanes] = scale * (
+        value = scale * (
             spread[rows, :]
             + mul_table(high_side[rows, :], low_side[rows, :], backward_high[...], backward_low[...])
         )
-
+        spread[rows, :] = value
+        here = pl.ds(g * unit, group * unit)
+        stores.append(pltpu.make_async_copy(spread.at[here], out.at[here], store_sem.at[g]))
+        stores[-1].start()
+    for store in stores:
+        store.wait()
+
+
+def output_kernel(
+    applied,
+    gather_high_far,
+    gather_low_far,
+    out,
+    here,
+    gather_high,
+    gather_low,
+    result,
+    fetch_sem,
+    store_sem,
+):
+    columns, y_orders, _, orders = out.shape
+    padded = gather_high.shape[0] // 2
+    span = gather_high.shape[1]
+    kept = min(y_orders, span // 2)
+    tables = [
+        pltpu.make_async_copy(gather_high_far, gather_high, fetch_sem.at[columns]),
+        pltpu.make_async_copy(gather_low_far, gather_low, fetch_sem.at[columns + 1]),
+    ]
+    fetches = []
+    for c in range(columns):
+        rows = pl.ds(c * span, span)
+        fetches.append(pltpu.make_async_copy(applied.at[rows], here.at[rows], fetch_sem.at[c]))
+    for copy in tables + fetches:
+        copy.start()
+    for copy in tables:
+        copy.wait()
     stores = []
     for c in range(columns):
-        high, low = split(state[c * 2 * lines : (c + 1) * 2 * lines, :lanes])
+        fetches[c].wait()
+        high, low = split(here[c * span : (c + 1) * span, :])
         value = (
             mul(gather_high[...], high) + mul(gather_high[...], low) + mul(gather_low[...], high)
         )
@@ -338,11 +389,11 @@
     symbol_pair = symbol_table(orders, pixels)
     spread_pair, gather_pair = line_tables(y_orders, lines)
     forward, backward, even, odd = order_tables(orders)
-    tables = [*spread_pair, *forward, *gather_pair, *backward, *even, *odd]
+    tables = [*spread_pair, *forward, *backward, *even, *odd]
     panel = mode_panel.transpose(0, 2, 1, 3)
-    result = pl.pallas_call(
+    applied = pl.pallas_call(
         apply_kernel,
-        out_shape=jax.ShapeDtypeStruct(panel.shape, jnp.float32),
+        out_shape=jax.ShapeDtypeStruct((total, lanes), jnp.float32),
         in_specs=[pl.BlockSpec(memory_space=pl.ANY)] * (5 + len(tables)),
         out_specs=pl.BlockSpec(memory_space=pl.ANY),
         scratch_shapes=[
@@ -359,17 +410,31 @@
             pltpu.VMEM((total, width), jnp.float32),
             pltpu.VMEM((total, width), jnp.bfloat16),
             pltpu.VMEM((total, width), jnp.bfloat16),
-            pltpu.VMEM(panel.shape, jnp.float32),
             pltpu.SemaphoreType.DMA((2 * CHUNKS + 3 + len(tables),)),
             pltpu.SemaphoreType.DMA((devices,)),
             pltpu.SemaphoreType.DMA((devices,)),
-            pltpu.SemaphoreType.DMA((columns,)),
+            pltpu.SemaphoreType.DMA((total // (2 * BLOCK),)),
         ],
         compiler_params=pltpu.CompilerParams(
             vmem_limit_bytes=VMEM_BYTES, collective_id=0, has_side_effects=True
         ),
         name="apply",
     )(materials, pixel_map, panel, *map(jnp.asarray, tables), *map(jnp.asarray, symbol_pair))
+    result = pl.pallas_call(
+        output_kernel,
+        out_shape=jax.ShapeDtypeStruct(panel.shape, jnp.float32),
+        in_specs=[pl.BlockSpec(memory_space=pl.ANY)] * 3,
+        out_specs=pl.BlockSpec(memory_space=pl.ANY),
+        scratch_shapes=[
+            pltpu.VMEM((total, lanes), jnp.float32),
+            *[pltpu.VMEM(table.shape, jnp.bfloat16) for table in gather_pair],
+            pltpu.VMEM(panel.shape, jnp.float32),
+            pltpu.SemaphoreType.DMA((columns + 2,)),
+            pltpu.SemaphoreType.DMA((columns,)),
+        ],
+        compiler_params=pltpu.CompilerParams(vmem_limit_bytes=VMEM_BYTES),
+        name="output",
+    )(applied, *map(jnp.asarray, gather_pair))
     return result.transpose(0, 2, 1, 3)
 
 

time: 23.8 us -> 24.4 us (1.025)
  Pallas kernels: 20.5 us -> 24.1 us
  local copies, waits for them, and re-layouts: 3.17 us -> 0 us
    pallas_call x1 -> x2, Pallas kernels: 20.5 us -> 24.1 us  [the longest x1 20.5 us: local(): pl.pallas_call(apply_kernel, out_shape=jax.ShapeDtypeStruct((total, lanes...]
    unnamed x1 -> x0, local copies, waits for them, and re-layouts: 3.17 us -> none
where the time goes in v3:
time: 24.4 us; the launch traced here: 24.1 us
  Pallas kernels  24.1 us (99%)
    pallas_call x1, Pallas kernels, local(): pl.pallas_call(apply_kernel, out_shape=jax.ShapeDtypeStruct((total, lanes...  20.5 us
    pallas_call x1, Pallas kernels, local(): pl.pallas_call(output_kernel, out_shape=jax.ShapeDtypeStruct(panel.shape,...  3.59 us

profile of v3, /device:TPU:1, one launch (start us, length us, event | category | flops | bytes accessed | tf_op | source)
XLA Modules:
  0.0 24.1 jit_solution(4660529441432180233)
XLA Ops:
  0.0 20.5 %apply.1.applied = f32[1024,256]{1,0:T(8,128)} custom-call(f32[4]{0:T(128)} %materials.1, s32[8,2048]{1,0:T(8,128)} %pixel_rows.1, f32[4,201,2,201]{3,2,1,0:T(2,128)} %bitcast.2, bf16[256,256]{1,0:T(8,128)(2,1)} %constant.28.clone.spread_high, bf16[256,256]{1,0:T(8,128)(2,1)} %constant.29.clone.spread_low, bf16[256,512]{1,0:T(8,128)(2,1)} %constant.30.clone.forward_high, ...), custom_call_target="tpu_custom_call" | custom-call | tf_op jit(solution)/shard_map/apply/pallas_call | solution.py:394
  20.5 3.6 %output.1 = f32[4,201,2,201]{3,2,1,0:T(2,128)} custom-call(f32[1024,256]{1,0:T(8,128)} %apply.1.applied, bf16[256,256]{1,0:T(8,128)(2,1)} %constant.40.clone.gather_high_far, bf16[256,256]{1,0:T(8,128)(2,1)} %constant.41.clone.gather_low_far), custom_call_target="tpu_custom_call" | custom-call | tf_op jit(solution)/shard_map/output/pallas_call | solution.py:423

commit v4 on v3

--- a/solution.py
+++ b/solution.py
@@ -59,15 +59,15 @@
     return split_table(forward), split_table(backward), split_table(even), split_table(odd)
 
 
-def line_tables(y_orders, lines):
+def line_tables(y_orders, lines, block):
     kept = min(y_orders, lines)
     padded = round_up(kept, BLOCK)
-    blocks = lines // BLOCK
+    blocks = lines // block
     angle = turns(np.arange(lines), np.arange(kept) - (y_orders - 1) // 2, lines)
-    cosine = np.zeros((blocks, BLOCK, padded))
-    sine = np.zeros((blocks, BLOCK, padded))
-    cosine[:, :, :kept] = np.cos(angle).reshape(blocks, BLOCK, kept)
-    sine[:, :, :kept] = np.sin(angle).reshape(blocks, BLOCK, kept)
+    cosine = np.zeros((blocks, block, padded))
+    sine = np.zeros((blocks, block, padded))
+    cosine[:, :, :kept] = np.cos(angle).reshape(blocks, block, kept)
+    sine[:, :, :kept] = np.sin(angle).reshape(blocks, block, kept)
     real = np.concatenate([cosine, -sine], axis=2)
     imag = np.concatenate([sine, cosine], axis=2)
     spread = np.stack([real, imag], axis=1).reshape(2 * lines, 2 * padded)
@@ -184,18 +184,9 @@
         copy.start()
     me = lax.axis_index("long")
     devices = lax.axis_size("long")
-    cores = 2
-    chips = devices // cores
-    chip = me // cores
-    core = lax.rem(me, cores)
-    sibling = chip * cores + (1 - core)
-
-    def twin(i):
-        return lax.rem(chip + i, chips) * cores + core
-
     barrier = pltpu.get_barrier_semaphore()
-    for peer in [sibling] + [twin(i) for i in range(1, chips)]:
-        pl.semaphore_signal(barrier, inc=1, device_id={"long": peer})
+    for i in range(1, devices):
+        pl.semaphore_signal(barrier, inc=1, device_id={"long": lax.rem(me + i, devices)})
     depth = table_high.shape[0] // CHUNKS
     fetched = []
     for i in range(CHUNKS):
@@ -214,35 +205,31 @@
     def slot(device):
         return landed.at[pl.ds(pl.multiple_of(device * count, count), count)]
 
-    def send(device, peer, i):
+    def send(device, i):
         return pltpu.make_async_remote_copy(
             src_ref=slot(device),
             dst_ref=slot(device),
             send_sem=send_sem.at[i],
-            recv_sem=recv_sem.at[i],
-            device_id={"long": peer},
+            recv_sem=recv_sem.at[device],
+            device_id={"long": lax.rem(me + i, devices)},
         )
 
     mine = slot(me)
     for copy in early[:2]:
         copy.wait()
     symbol_of(scalars, pixels[...], (high_table, low_table), fetched, mine)
-    pl.semaphore_wait(barrier, chips)
-    sent = [send(me, twin(i), i) for i in range(1, chips)]
-    handed = [send(me, sibling, chips)]
-    for copy in sent[::-1] + handed:
+    pl.semaphore_wait(barrier, devices - 1)
+    sent = [send(me, i) for i in range(1, devices)]
+    for copy in sent:
         copy.start()
-
-    def hand_on():
-        for i in range(1, chips):
-            sent[i - 1].wait()
-            handed.append(send(twin(chips - i), sibling, chips + i))
-            handed[-1].start()
 
     columns, y_orders, _, orders = panel.shape
     lines = landed.shape[0]
     kept = min(y_orders, lines)
     padded = spread_high.shape[1] // 2
+    block = BLOCK // columns
+    blocks = lines // block
+    unit = 2 * BLOCK
     folded[...] = jnp.zeros(folded.shape, jnp.float32)
     for copy in early[2:]:
         copy.wait()
@@ -259,75 +246,82 @@
             + mul(spread_high_here[...], low)
             + mul(spread_low_here[...], high)
         )
-        rows = slice(c * 2 * lines, (c + 1) * 2 * lines)
-        spread[rows, :] = value
         high, low = split(value)
-        start[rows, :] = mul_table(high, low, forward_high_here[...], forward_low_here[...])
-        if c == max(columns - 2, 0):
-            hand_on()
-
-    for copy in handed:
-        copy.wait()
+        begun = mul_table(high, low, forward_high_here[...], forward_low_here[...])
+        for b in range(blocks):
+            rows = slice(b * unit + c * 2 * block, b * unit + (c + 1) * 2 * block)
+            spread[rows, :] = value[b * 2 * block : (b + 1) * 2 * block, :]
+            start[rows, :] = begun[b * 2 * block : (b + 1) * 2 * block, :]
+
     symbol = landed
     for copy in late:
         copy.wait()
 
     width = symbol.shape[1]
     lanes = width // 2
-    blocks = lines // BLOCK
-    unit = 2 * BLOCK
-    units = columns * blocks
-    group = 2 if units % 2 == 0 else 1
-
-    def weigh(u, state):
-        real = slice(u * unit, u * unit + BLOCK)
-        imag = slice(u * unit + BLOCK, (u + 1) * unit)
-        here = slice((u % blocks) * BLOCK, (u % blocks + 1) * BLOCK)
+    group = 2 if blocks % 2 == 0 else 1
+    scale = scale_of(scalars, (1, lanes))
+
+    def weigh(b, state):
+        here = slice(b * block, (b + 1) * block)
         p = symbol[here, :lanes]
         q = symbol[here, lanes:]
-        even_real = state[real, :lanes]
-        even_imag = state[imag, :lanes]
-        odd_real = state[real, lanes:]
-        odd_imag = state[imag, lanes:]
-        for rows, cols, value in (
-            (real, slice(0, lanes), p * even_real + q * odd_imag),
-            (imag, slice(0, lanes), p * even_imag - q * odd_real),
-            (real, slice(lanes, width), p * odd_real - q * even_imag),
-            (imag, slice(lanes, width), p * odd_imag + q * even_real),
-        ):
-            high, low = split(value)
-            high_side[rows, cols] = high
-            low_side[rows, cols] = low
-
-    def sweep(source):
-        for g in range(0, units, group):
-            rows = slice(g * unit, (g + group) * unit)
-            for u in range(g, g + group):
-                weigh(u, source)
-            state[rows, :lanes] = start[rows, :lanes] + mul_table(
-                high_side[rows, :lanes], low_side[rows, :lanes], even_high[...], even_low[...]
+        for c in range(columns):
+            first = b * unit + c * 2 * block
+            real = slice(first, first + block)
+            imag = slice(first + block, first + 2 * block)
+            even_real = state[real, :lanes]
+            even_imag = state[imag, :lanes]
+            odd_real = state[real, lanes:]
+            odd_imag = state[imag, lanes:]
+            for rows, cols, value in (
+                (real, slice(0, lanes), p * even_real + q * odd_imag),
+                (imag, slice(0, lanes), p * even_imag - q * odd_real),
+                (real, slice(lanes, width), p * odd_real - q * even_imag),
+                (imag, slice(lanes, width), p * odd_imag + q * even_real),
+            ):
+                high, low = split(value)
+                high_side[rows, cols] = high
+                low_side[rows, cols] = low
+
+    def sweep(b, source):
+        weigh(b, source)
+        rows = slice(b * unit, (b + 1) * unit)
+        state[rows, :lanes] = start[rows, :lanes] + mul_table(
+            high_side[rows, :lanes], low_side[rows, :lanes], even_high[...], even_low[...]
+        )
+        state[rows, lanes:] = start[rows, lanes:] + mul_table(
+            high_side[rows, lanes:], low_side[rows, lanes:], odd_high[...], odd_low[...]
+        )
+
+    def arrive(device):
+        @pl.when(device != me)
+        def _():
+            send(device, 1).wait_recv()
+
+    stores = []
+    arrived = 0
+    for g in range(0, blocks, group):
+        while arrived * count < (g + group) * block:
+            arrive(arrived)
+            arrived += 1
+        for i in range(2**NS_ITERS - 2):
+            for b in range(g, g + group):
+                sweep(b, state if i else start)
+        for b in range(g, g + group):
+            weigh(b, state)
+            rows = slice(b * unit, (b + 1) * unit)
+            spread[rows, :] = scale * (
+                spread[rows, :]
+                + mul_table(
+                    high_side[rows, :], low_side[rows, :], backward_high[...], backward_low[...]
+                )
             )
-            state[rows, lanes:] = start[rows, lanes:] + mul_table(
-                high_side[rows, lanes:], low_side[rows, lanes:], odd_high[...], odd_low[...]
-            )
-
-    for i in range(2**NS_ITERS - 2):
-        sweep(state if i else start)
-
-    scale = scale_of(scalars, (1, lanes))
-    stores = []
-    for g in range(0, units, group):
-        rows = slice(g * unit, (g + group) * unit)
-        for u in range(g, g + group):
-            weigh(u, state)
-        value = scale * (
-            spread[rows, :]
-            + mul_table(high_side[rows, :], low_side[rows, :], backward_high[...], backward_low[...])
-        )
-        spread[rows, :] = value
-        here = pl.ds(g * unit, group * unit)
-        stores.append(pltpu.make_async_copy(spread.at[here], out.at[here], store_sem.at[g]))
-        stores[-1].start()
+            here = pl.ds(b * unit, unit)
+            stores.append(pltpu.make_async_copy(spread.at[here], out.at[here], store_sem.at[b]))
+            stores[-1].start()
+    for copy in sent:
+        copy.wait_send()
     for store in stores:
         store.wait()
 
@@ -348,22 +342,26 @@
     padded = gather_high.shape[0] // 2
     span = gather_high.shape[1]
     kept = min(y_orders, span // 2)
+    block = BLOCK // columns
+    blocks = span // (2 * block)
+    unit = 2 * BLOCK
     tables = [
-        pltpu.make_async_copy(gather_high_far, gather_high, fetch_sem.at[columns]),
-        pltpu.make_async_copy(gather_low_far, gather_low, fetch_sem.at[columns + 1]),
+        pltpu.make_async_copy(gather_high_far, gather_high, fetch_sem.at[blocks]),
+        pltpu.make_async_copy(gather_low_far, gather_low, fetch_sem.at[blocks + 1]),
     ]
     fetches = []
-    for c in range(columns):
-        rows = pl.ds(c * span, span)
-        fetches.append(pltpu.make_async_copy(applied.at[rows], here.at[rows], fetch_sem.at[c]))
+    for b in range(blocks):
+        rows = pl.ds(b * unit, unit)
+        fetches.append(pltpu.make_async_copy(applied.at[rows], here.at[rows], fetch_sem.at[b]))
     for copy in tables + fetches:
         copy.start()
-    for copy in tables:
+    for copy in tables + fetches:
         copy.wait()
     stores = []
     for c in range(columns):
-        fetches[c].wait()
-        high, low = split(here[c * span : (c + 1) * span, :])
+        first = c * 2 * block
+        pieces = [here[b * unit + first : b * unit + first + 2 * block, :] for b in range(blocks)]
+        high, low = split(jnp.concatenate(pieces, axis=0))
         value = (
             mul(gather_high[...], high) + mul(gather_high[...], low) + mul(gather_low[...], high)
         )
@@ -387,7 +385,7 @@
     width = 2 * lanes
     total = columns * 2 * lines
     symbol_pair = symbol_table(orders, pixels)
-    spread_pair, gather_pair = line_tables(y_orders, lines)
+    spread_pair, gather_pair = line_tables(y_orders, lines, BLOCK // columns)
     forward, backward, even, odd = order_tables(orders)
     tables = [*spread_pair, *forward, *backward, *even, *odd]
     panel = mode_panel.transpose(0, 2, 1, 3)
@@ -429,7 +427,7 @@
             pltpu.VMEM((total, lanes), jnp.float32),
             *[pltpu.VMEM(table.shape, jnp.bfloat16) for table in gather_pair],
             pltpu.VMEM(panel.shape, jnp.float32),
-            pltpu.SemaphoreType.DMA((columns + 2,)),
+            pltpu.SemaphoreType.DMA((total // (2 * BLOCK) + 2,)),
             pltpu.SemaphoreType.DMA((columns,)),
         ],
         compiler_params=pltpu.CompilerParams(vmem_limit_bytes=VMEM_BYTES),

time: 24.4 us -> 22.6 us (0.926)
  the two profiles are of different devices: /device:TPU:1 before, /device:TPU:31 now
where the time goes in v4:
time: 22.6 us; the launch traced here: 22.4 us
  Pallas kernels  22.4 us (99%)
    pallas_call x1, Pallas kernels, local(): pl.pallas_call(apply_kernel, out_shape=jax.ShapeDtypeStruct((total, lanes...  19.2 us
    pallas_call x1, Pallas kernels, local(): pl.pallas_call(output_kernel, out_shape=jax.ShapeDtypeStruct(panel.shape,...  3.18 us

profile of v4, /device:TPU:31, one launch (start us, length us, event | category | flops | bytes accessed | tf_op | source)
XLA Modules:
  0.0 22.4 jit_solution(12264137176721854341)
XLA Ops:
  0.0 19.2 %apply.1.applied = f32[1024,256]{1,0:T(8,128)} custom-call(f32[4]{0:T(128)} %materials.1, s32[8,2048]{1,0:T(8,128)} %pixel_rows.1, f32[4,201,2,201]{3,2,1,0:T(2,128)} %bitcast.2, bf16[256,256]{1,0:T(8,128)(2,1)} %constant.28.clone.spread_high, bf16[256,256]{1,0:T(8,128)(2,1)} %constant.29.clone.spread_low, bf16[256,512]{1,0:T(8,128)(2,1)} %constant.30.clone.forward_high, ...), custom_call_target="tpu_custom_call" | custom-call | tf_op jit(solution)/shard_map/apply/pallas_call | solution.py:392
  19.2 3.2 %output.1 = f32[4,201,2,201]{3,2,1,0:T(2,128)} custom-call(f32[1024,256]{1,0:T(8,128)} %apply.1.applied, bf16[256,256]{1,0:T(8,128)(2,1)} %constant.40.clone.gather_high_far, bf16[256,256]{1,0:T(8,128)(2,1)} %constant.41.clone.gather_low_far), custom_call_target="tpu_custom_call" | custom-call | tf_op jit(solution)/shard_map/output/pallas_call | solution.py:421

commit v5 on v4

--- a/solution.py
+++ b/solution.py
@@ -299,12 +299,13 @@
         def _():
             send(device, 1).wait_recv()
 
-    stores = []
-    arrived = 0
-    for g in range(0, blocks, group):
-        while arrived * count < (g + group) * block:
-            arrive(arrived)
-            arrived += 1
+    def store(b):
+        here = pl.ds(b * unit, unit)
+        return pltpu.make_async_copy(spread.at[here], out.at[here], store_sem.at[b])
+
+    def run(g):
+        for device in range(g * block // count, (g + group) * block // count):
+            arrive(device)
         for i in range(2**NS_ITERS - 2):
             for b in range(g, g + group):
                 sweep(b, state if i else start)
@@ -317,13 +318,25 @@
                     high_side[rows, :], low_side[rows, :], backward_high[...], backward_low[...]
                 )
             )
-            here = pl.ds(b * unit, unit)
-            stores.append(pltpu.make_async_copy(spread.at[here], out.at[here], store_sem.at[b]))
-            stores[-1].start()
+            store(b).start()
+
+    lower = me < devices // 2
+
+    @pl.when(lower)
+    def _():
+        run(0)
+
+    for g in range(group, blocks, group):
+        run(g)
+
+    @pl.when(jnp.logical_not(lower))
+    def _():
+        run(0)
+
     for copy in sent:
         copy.wait_send()
-    for store in stores:
-        store.wait()
+    for b in range(blocks):
+        store(b).wait()
 
 
 def output_kernel(

time: 22.6 us -> 22.6 us (level)
  the two profiles are of different devices: /device:TPU:31 before, /device:TPU:1 now
where the time goes in v5:
time: 22.6 us; the launch traced here: 22.4 us
  Pallas kernels  22.3 us (99%)
    pallas_call x1, Pallas kernels, local(): pl.pallas_call(apply_kernel, out_shape=jax.ShapeDtypeStruct((total, lanes...  19.1 us
    pallas_call x1, Pallas kernels, local(): pl.pallas_call(output_kernel, out_shape=jax.ShapeDtypeStruct(panel.shape,...  3.18 us

profile of v5, /device:TPU:1, one launch (start us, length us, event | category | flops | bytes accessed | tf_op | source)
XLA Modules:
  0.0 22.4 jit_solution(8064879193979444135)
XLA Ops:
  0.0 19.1 %apply.1.applied = f32[1024,256]{1,0:T(8,128)} custom-call(f32[4]{0:T(128)} %materials.1, s32[8,2048]{1,0:T(8,128)} %pixel_rows.1, f32[4,201,2,201]{3,2,1,0:T(2,128)} %bitcast.2, bf16[256,256]{1,0:T(8,128)(2,1)} %constant.28.clone.spread_high, bf16[256,256]{1,0:T(8,128)(2,1)} %constant.29.clone.spread_low, bf16[256,512]{1,0:T(8,128)(2,1)} %constant.30.clone.forward_high, ...), custom_call_target="tpu_custom_call" | custom-call | tf_op jit(solution)/shard_map/apply/pallas_call | solution.py:405
  19.1 3.2 %output.1 = f32[4,201,2,201]{3,2,1,0:T(2,128)} custom-call(f32[1024,256]{1,0:T(8,128)} %apply.1.applied, bf16[256,256]{1,0:T(8,128)(2,1)} %constant.40.clone.gather_high_far, bf16[256,256]{1,0:T(8,128)(2,1)} %constant.41.clone.gather_low_far), custom_call_target="tpu_custom_call" | custom-call | tf_op jit(solution)/shard_map/output/pallas_call | solution.py:434
